TPU v7x, 32 devices: a whole 2x2x4 slice. The times are simulated.
32 devices in a mesh: gx: 4 (over y, core), gy: 8 (over z, x).
Axes of the slice: x: 2, y: 2, z: 4, core: 2. Of those that a mesh axis runs over, the one named last changes fastest.
Arguments:
- tiles: float32 [2, 3, 16384, 128], P(None, None, ('gx', 'gy')), may hold values from -6 to 6
- tile_owner: int32 [16384, 1], P(('gx', 'gy')), may hold values from 0 to 31; in each aligned block of 512 rows (0 to 511, 512 to 1023, ...) at most 32 rows name the same one
- tile_slot: int32 [16384], P(('gx', 'gy')), may hold values from 0 to 1023
- tile_count: int32 [32], P(('gx', 'gy')), may hold values from 384 to 512, as said below
- green: float32 [2, 6, 1, 2048, 2048], P(None, None, None, ('gx', 'gy')), may hold values from -6 to 6
Outputs:
- field_hat: float32 [2, 3, 1, 2048, 2048], P(None, None, None, ('gx', 'gy'))
Inputs may be any that keep to these rules, and one draw needn't show every extreme that they name: `tile_owner`: within the 512 entries of one device, live or not, no owner is named by more than 32; that many is reached. `tile_count`: some device has all 512 entries live.
All inputs are finite; a program needn't handle non-finite values.
Results may differ from a plain program's by a relative error of at most 0.00007.
Values sent between devices are 32-bit elements; how exact they have to be, the bound alone decides.
No kernel may reach another device: no remote copies, remote signals or barrier semaphores. Data moves between devices by JAX's collectives and lax.ppermute only.
A program may use at most 128 MiB of HBM per device.

v0:
```python
import math

import jax
import jax.numpy as jnp
from jax import lax
from jax.sharding import PartitionSpec as P

pair_index = ((0, 3, 4), (3, 1, 5), (4, 5, 2))


def angle_table(length):
    index = jnp.arange(length, dtype=jnp.int32)
    products = index[:, None] * index[None, :] % length
    angles = 2.0 * math.pi / length * products.astype(jnp.float32)
    return (jnp.cos(angles), jnp.sin(angles))


def table_first(table, data):
    return lax.dot_general(table, data, (((1,), (1,)), ((), ())), precision=lax.Precision.HIGHEST)


def across_sources(data, table):
    return lax.dot_general(
        data, table, (((0, 4), (0, 1)), ((), ())), precision=lax.Precision.HIGHEST
    )


def per_device(tiles, tile_owner, tile_slot, tile_count, green):
    count_gx = lax.axis_size("gx")
    count_gy = lax.axis_size("gy")
    devices = count_gx * count_gy
    tile_total = tiles.shape[2]
    tile_len = tiles.shape[3]
    planes = green.shape[2]
    y_local = green.shape[3]
    x_cells = green.shape[4]
    y_cells = y_local * devices
    x_local = x_cells // devices
    slots_total = planes * x_local * (y_cells // tile_len)
    per_owner = max(2, 2 * tile_total // devices)
    owner = tile_owner[:, 0]
    position = jnp.arange(tile_total, dtype=jnp.int32)
    is_live = position < tile_count[0]
    earlier = (
        (owner[:, None] == owner[None, :])
        & is_live[None, :]
        & (position[None, :] < position[:, None])
    )
    tile_rank = jnp.sum(earlier.astype(jnp.int32), axis=1)
    target = jnp.where(is_live, owner * per_owner + tile_rank, devices * per_owner)
    outgoing = jnp.zeros((2, 3, devices * per_owner, tile_len), jnp.float32)
    outgoing = outgoing.at[:, :, target, :].set(tiles, mode="drop")
    places = jnp.full((devices * per_owner,), -1, jnp.int32).at[target].set(tile_slot, mode="drop")
    arriving, arrived_slot = (
        lax.all_to_all(
            outgoing.reshape(2, 3, devices, per_owner, tile_len),
            ("gx", "gy"),
            split_axis=2,
            concat_axis=2,
            tiled=True,
        ),
        lax.all_to_all(
            places.reshape(1, 1, devices, per_owner),
            ("gx", "gy"),
            split_axis=2,
            concat_axis=2,
            tiled=True,
        ),
    )
    arriving = arriving.reshape(2, 3, devices * per_owner, tile_len)
    arrived_slot = arrived_slot.reshape(devices * per_owner)
    landing = jnp.where(arrived_slot < 0, slots_total, arrived_slot)
    slab_field = jnp.zeros((2, 3, slots_total, tile_len), jnp.float32)
    slab_field = slab_field.at[:, :, landing, :].add(arriving, mode="drop")
    row_count = 3 * planes * x_local
    real_rows = slab_field[0].reshape(row_count, y_cells)
    imag_rows = slab_field[1].reshape(row_count, y_cells)
    cos_y, sin_y = angle_table(y_cells)
    y_scale = 1.0 / math.sqrt(y_cells)
    real_y = (table_first(cos_y, real_rows) + table_first(sin_y, imag_rows)) * y_scale
    imag_y = (table_first(cos_y, imag_rows) - table_first(sin_y, real_rows)) * y_scale
    halfway = jnp.stack([real_y, imag_y])
    moved = lax.all_to_all(halfway, ("gx", "gy"), split_axis=1, concat_axis=1, tiled=True)
    moved = moved.reshape(2, devices, y_local, 3, planes, x_local)
    cos_x, sin_x = angle_table(x_cells)
    cos_x = cos_x.reshape(devices, x_local, x_cells)
    sin_x = sin_x.reshape(devices, x_local, x_cells)
    x_scale = 1.0 / math.sqrt(x_cells)
    real_x = (across_sources(moved[0], cos_x) + across_sources(moved[1], sin_x)) * x_scale
    imag_x = (across_sources(moved[1], cos_x) - across_sources(moved[0], sin_x)) * x_scale
    spectrum = jnp.stack([real_x, imag_x]).transpose(0, 2, 3, 1, 4)
    mixed_real = []
    mixed_imag = []
    for row_comp in range(3):
        real_sum = jnp.zeros_like(spectrum[0, 0])
        imag_sum = jnp.zeros_like(spectrum[0, 0])
        for col_comp in range(3):
            tensor_entry = pair_index[row_comp][col_comp]
            green_real = green[0, tensor_entry]
            green_imag = green[1, tensor_entry]
            real_sum = (
                real_sum + green_real * spectrum[0, col_comp] - green_imag * spectrum[1, col_comp]
            )
            imag_sum = (
                imag_sum + green_real * spectrum[1, col_comp] + green_imag * spectrum[0, col_comp]
            )
        mixed_real.append(real_sum)
        mixed_imag.append(imag_sum)
    return jnp.stack([jnp.stack(mixed_real), jnp.stack(mixed_imag)])


def solution(mesh):
    in_specs = (
        P(None, None, ("gx", "gy"), None),
        P(("gx", "gy"), None),
        P(("gx", "gy")),
        P(("gx", "gy")),
        P(None, None, None, ("gx", "gy"), None),
    )
    out_specs = P(None, None, None, ("gx", "gy"), None)
    return jax.shard_map(
        per_device, mesh=mesh, in_specs=in_specs, out_specs=out_specs, check_vma=False
    )
```

profile of v0, /device:TPU:0, one launch (start us, length us, event | category | flops | bytes accessed | tf_op | source)
XLA Modules:
  0.0 948.4 jit_solution(15265849520693694890)
XLA Ops:
  0.7 1.0 convert_reduce_fusion
  1.7 0.7 compare_select_fusion.2
  2.4 2.6 scatter_custom_fusion
  5.0 0.7 reshape.1141
  5.7 7.3 all-to-all-start
  13.0 3.8 copy.74
  16.7 0.8 broadcast.319.clone
  17.6 47.1 %scatter_fusion = f32[2,3,1024,128]{3,0,2,1:T(2,128)S(1)} fusion(f32[2,3,1024,128]{3,0,2,1:T(2,128)S(1)} %broadcast.319.clone, s32[512]{0:T(512)S(1)} %bitcast.199, f32[512,2,3,128]{3,1,2,0:T(2,128)} %copy.74), kind=kCustom, calls=%fused_computation.1 | custom fusion | bytes 4720640 | tf_op jit(solution)/shard_map/scatter | solution.py:52
  64.7 1.9 copy.75
  66.6 0.0 all-to-all-done
  66.6 6.3 all-to-all-start.1
  72.9 61.7 %fusion.164 = f32[2048,2048]{1,0:T(8,128)} fusion(), kind=kLoop, calls=%fused_computation.32.clone.1.clone | loop fusion | flops 58720256 | bytes 16777216 | tf_op jit(solution)/shard_map/dot_general | solution.py:19
  134.6 62.3 %fusion.166 = f32[2048,2048]{1,0:T(8,128)} fusion(), kind=kLoop, calls=%fused_computation.31.clone.1.clone.clone.clone.clone.clone.clone.clone.1 | loop fusion | flops 58720256 | bytes 16777216 | tf_op jit(solution)/shard_map/dot_general | solution.py:19
  197.0 61.8 %fusion.162 = f32[2048,2048]{1,0:T(8,128)} fusion(), kind=kLoop, calls=%fused_computation.32.clone.clone.1 | loop fusion | flops 58720256 | bytes 16777216 | tf_op jit(solution)/shard_map/dot_general | solution.py:19
  258.7 62.3 %fusion.168 = f32[2048,2048]{1,0:T(8,128)} fusion(), kind=kLoop, calls=%fused_computation.31.clone.clone.clone.clone.clone.clone.clone.clone.1 | loop fusion | flops 58720256 | bytes 16777216 | tf_op jit(solution)/shard_map/dot_general | solution.py:19
  321.0 0.6 broadcast.457
  321.6 0.7 reduce.11
  322.3 0.1 reshape.1142
  322.4 0.0 all-to-all-done.1
  322.4 0.4 copy.76
  322.8 4.1 copy.77
  326.9 0.8 broadcast.319
  327.7 85.2 %scatter_fusion.1 = f32[2,3,1024,128]{3,0,2,1:T(2,128)S(1)} fusion(f32[2,3,1024,128]{3,0,2,1:T(2,128)S(1)} %broadcast.319, s32[1024]{0:T(1024)S(1)} %bitcast.197, f32[1024,2,3,128]{3,1,2,0:T(2,128)} %copy.77), kind=kCustom, calls=%fused_computation.2 | custom fusion | flops 786432 | bytes 9441280 | tf_op jit(solution)/shard_map/scatter-add | solution.py:74
  413.0 10.2 %slice_reduce_fusion.1 = (f32[3,1024,128]{2,1,0:T(8,128)}, f32[3,1024,128]{2,1,0:T(8,128)}) fusion(f32[2,3,1024,128]{3,0,2,1:T(2,128)S(1)} %scatter_fusion.1), kind=kLoop, calls=%fused_computation.59 | loop fusion | bytes 6291456 | tf_op jit(solution)/shard_map/slice | solution.py:76
  423.2 1.5 reshape_squeeze.6
  424.7 1.5 reshape_squeeze.7
  426.2 20.1 %fusion.30 = f32[2048,192]{0,1:T(8,128)S(1)} fusion(f32[192,2048]{1,0:T(8,128)S(1)} %reshape_squeeze.6, f32[2048,2048]{1,0:T(8,128)} %fusion.164), kind=kOutput, calls=%fused_computation.34 | convolution fusion | flops 9663676416 | bytes 19922944 | tf_op jit(solution)/shard_map/dot_general | solution.py:19
  446.3 0.0 slice-start
  446.3 0.0 slice-start.1
  446.3 20.2 %fusion.28 = f32[2048,192]{0,1:T(8,128)S(1)} fusion(f32[192,2048]{1,0:T(8,128)S(1)} %reshape_squeeze.7, f32[2048,2048]{1,0:T(8,128)} %fusion.162), kind=kOutput, calls=%fused_computation.33 | convolution fusion | flops 9663676416 | bytes 19922944 | tf_op jit(solution)/shard_map/dot_general | solution.py:19
  466.5 0.0 slice-start.2
  466.5 0.0 slice-start.3
  466.5 20.4 %fusion.74 = f32[1,2048,192]{1,2,0:T(8,128)S(1)} fusion(f32[2048,192]{0,1:T(8,128)S(1)} %fusion.30, f32[192,2048]{1,0:T(8,128)S(1)} %reshape_squeeze.7, f32[2048,2048]{1,0:T(8,128)} %fusion.166), kind=kOutput, calls=%fused_computation.54 | convolution fusion | flops 9664462848 | bytes 21495808 | tf_op jit(solution)/shard_map/dot_general | solution.py:19
  486.9 0.0 slice-done
  486.9 0.0 slice-done.1
  486.9 0.0 slice-done.2
  487.0 0.0 slice-done.3
  487.0 18.0 %fusion.83 = f32[1,2048,192]{1,2,0:T(8,128)S(1)} fusion(f32[2048,192]{0,1:T(8,128)S(1)} %fusion.28, f32[192,2048]{1,0:T(8,128)S(1)} %reshape_squeeze.6, f32[2048,2048]{1,0:T(8,128)S(1)} %bitcast.190), kind=kOutput, calls=%fused_computation.57 | convolution fusion | flops 9664462848 | bytes 21495808 | tf_op jit(solution)/shard_map/dot_general | solution.py:19
  504.9 0.3 pad_maximum_fusion
  505.3 4.5 copy.78
  509.8 14.2 %all-to-all-start.2 = ((f32[2,2048,192]{2,0,1:T(2,128)}), f32[2,2048,192]{2,0,1:T(2,128)}, u32[]{:S(2)}, u32[]{:S(2)}) async-start(f32[2,2048,192]{2,0,1:T(2,128)} %copy.78), calls=%async_computation.2 | async-start | bytes 8388608 | tf_op jit(solution)/shard_map/all_to_all | solution.py:83
  524.0 95.1 %all-to-all-done.2 = f32[2,2048,192]{2,0,1:T(2,128)} async-done(((f32[2,2048,192]{2,0,1:T(2,128)}), f32[2,2048,192]{2,0,1:T(2,128)}, u32[]{:S(2)}, u32[]{:S(2)}) %all-to-all-start.2) | async-done | bytes 3145760 | tf_op jit(solution)/shard_map/all_to_all | solution.py:83
  619.1 7.6 fusion.135
  626.7 5.9 copy.79
  632.6 3.6 reshape.1145
  636.3 3.5 copy.80
  639.8 3.7 reshape.1146
  643.6 0.0 copy-done
  643.6 73.9 %fusion.36 = f32[64,3,2048]{2,0,1:T(8,128)S(1)} fusion(f32[32,64,3,64]{1,0,3,2:T(8,128)S(1)} %copy-done, s32[32,64]{0,1:T(8,128)S(1)} %multiply_add_fusion), kind=kOutput, calls=%fused_computation.40 | convolution fusion | flops 9722396672 | bytes 3153920 | tf_op jit(solution)/shard_map/dot_general | solution.py:23
  717.5 74.1 %fusion.39 = f32[64,3,2048]{2,0,1:T(8,128)S(1)} fusion(f32[32,64,3,64]{1,0,3,2:T(8,128)S(1)} %copy-done.1, s32[32,64]{0,1:T(8,128)S(1)} %multiply_add_fusion), kind=kOutput, calls=%fused_computation.41 | convolution fusion | flops 9722396672 | bytes 3153920 | tf_op jit(solution)/shard_map/dot_general | solution.py:23
  791.6 0.0 slice-start.4
  791.6 74.7 %fusion.59 = f32[1,64,3,1,2048]{4,1,2,3,0:T(8,128)S(1)} fusion(f32[64,3,2048]{2,0,1:T(8,128)S(1)} %fusion.36, f32[32,64,3,64]{1,0,3,2:T(8,128)S(1)} %copy-done.1, s32[32,64]{0,1:T(8,128)S(1)} %multiply_add_fusion), kind=kOutput, calls=%fused_computation.49 | convolution fusion | flops 9723183104 | bytes 4726784 | tf_op jit(solution)/shard_map/dot_general | solution.py:23
  866.4 0.0 slice-start.5
  866.4 75.1 %fusion.65 = f32[1,64,3,1,2048]{4,1,2,3,0:T(8,128)S(1)} fusion(f32[64,3,2048]{2,0,1:T(8,128)S(1)} %fusion.39, f32[32,64,3,64]{1,0,3,2:T(8,128)S(1)} %copy-done, s32[32,64]{0,1:T(8,128)S(1)} %multiply_add_fusion), kind=kOutput, calls=%fused_computation.51 | convolution fusion | flops 9723183104 | bytes 4726784 | tf_op jit(solution)/shard_map/dot_general | solution.py:23
  941.5 0.8 fusion.48
  942.3 0.6 fusion.90
  942.9 0.6 fusion.92
  943.5 0.6 fusion.94
  944.0 0.6 fusion.97
  944.6 0.6 fusion.100
  945.2 0.6 fusion.87
  945.7 0.1 maximum_bitcast_fusion.1
  945.9 0.1 maximum_bitcast_fusion.2
  946.0 1.9 maximum_bitcast_fusion
  (10 shorter events, 0.0 us)
Async XLA Ops:
  5.7 60.9 %all-to-all-start = ((s32[1,1,32,32]{3,1,0,2:T(1,128)}), s32[1,1,32,32]{3,1,0,2:T(1,128)S(1)}, u32[]{:S(2)}, u32[]{:S(2)}) async-start(s32[1,1,32,32]{3,1,0,2:T(1,128)} %reshape.1141), calls=%async_computation | async-start | bytes 32768 | tf_op jit(solution)/shard_map/all_to_all | solution.py:62
  66.6 255.8 %all-to-all-start.1 = ((f32[2,3,32,32,128]{4,0,3,1,2:T(2,128)}), f32[2,3,32,32,128]{4,0,3,1,2:T(2,128)S(1)}, u32[]{:S(2)}, u32[]{:S(2)}) async-start(f32[2,3,32,32,128]{4,0,3,1,2:T(2,128)} %copy.75), calls=%async_computation.1 | async-start | bytes 6291456 | tf_op jit(solution)/shard_map/all_to_all | solution.py:55
  446.3 40.6 %slice-start = ((s8[16777216]{0:T(1024)(128)(4,1)}), s8[4194304]{0:T(1024)(128)(4,1)S(1)}, s32[]{:S(2)}) async-start(s8[16777216]{0:T(1024)(128)(4,1)} %bitcast.189), calls=%async_computation.3 | async-start | bytes 8388608
  446.3 40.6 %slice-start.1 = ((s8[16777216]{0:T(1024)(128)(4,1)}), s8[4194304]{0:T(1024)(128)(4,1)S(1)}, s32[]{:S(2)}) async-start(s8[16777216]{0:T(1024)(128)(4,1)} %bitcast.189), calls=%async_computation.4 | async-start | bytes 8388608
  466.5 20.4 %slice-start.2 = ((s8[16777216]{0:T(1024)(128)(4,1)}), s8[4194304]{0:T(1024)(128)(4,1)S(1)}, s32[]{:S(2)}) async-start(s8[16777216]{0:T(1024)(128)(4,1)} %bitcast.189), calls=%async_computation.5 | async-start | bytes 8388608
  466.5 20.4 %slice-start.3 = ((s8[16777216]{0:T(1024)(128)(4,1)}), s8[4194304]{0:T(1024)(128)(4,1)S(1)}, s32[]{:S(2)}) async-start(s8[16777216]{0:T(1024)(128)(4,1)} %bitcast.189), calls=%async_computation.6 | async-start | bytes 8388608
  509.8 109.3 %all-to-all-start.2 = ((f32[2,2048,192]{2,0,1:T(2,128)}), f32[2,2048,192]{2,0,1:T(2,128)}, u32[]{:S(2)}, u32[]{:S(2)}) async-start(f32[2,2048,192]{2,0,1:T(2,128)} %copy.78), calls=%async_computation.2 | async-start | bytes 8388608 | tf_op jit(solution)/shard_map/all_to_all | solution.py:83
  639.8 3.8 copy-start
  643.6 73.9 %copy-start.1 = (f32[32,64,3,64]{1,0,3,2:T(8,128)S(1)}, f32[32,64,3,64]{1,0,3,2:T(8,128)}, u32[]{:S(2)}) copy-start(f32[32,64,3,64]{1,0,3,2:T(8,128)} %reshape.1146) | copy-start | bytes 4718596
  791.6 150.7 %slice-start.4 = ((s8[6291456]{0:T(1024)(128)(4,1)}), s8[4194304]{0:T(1024)(128)(4,1)S(1)}, s32[]{:S(2)}) async-start(s8[6291456]{0:T(1024)(128)(4,1)} %bitcast.191), calls=%async_computation.7 | async-start | bytes 8388608
  866.4 75.9 %slice-start.5 = ((s8[6291456]{0:T(1024)(128)(4,1)}), s8[2097152]{0:T(1024)(128)(4,1)S(1)}, s32[]{:S(2)}) async-start(s8[6291456]{0:T(1024)(128)(4,1)} %bitcast.191), calls=%async_computation.8 | async-start | bytes 4194304
where the time goes:
time: 958 us; the launch traced here: 948 us
  matrix products  376 us (39%)
  other arithmetic  342 us (36%)
  local copies, waits for them, and re-layouts  105 us (11%)
  waiting for transfers between devices  95.1 us (10%)
  starting transfers between devices  27.8 us (3%)
    dot_general x4, matrix products, across_sources(): lax.dot_general(data, table, (((0, 4), (0, 1)), ((), ())), precision=lax....  298 us
    dot_general x4, other arithmetic, table_first(): lax.dot_general(table, data, (((1,), (1,)), ((), ())), precision=lax.Prec...  248 us
    all_to_all x1, waiting for transfers between devices, per_device(): lax.all_to_all(halfway, ('gx', 'gy'), split_axis=1, concat_axis=1, tiled=...  95.1 us
    scatter-add x1, other arithmetic, per_device(): slab_field = slab_field.at[:, :, landing, :].add(arriving, mode='drop')  85.2 us
    dot_general x4, matrix products, table_first(): lax.dot_general(table, data, (((1,), (1,)), ((), ())), precision=lax.Prec...  78.6 us
    scatter x1, local copies, waits for them, and re-layouts, per_device(): outgoing = outgoing.at[:, :, target, :].set(tiles, mode='drop')  47.1 us
  transfers between devices with their start and end apart: 3, of which 1 were waited for; matrix products, arithmetic and copies ran while one was open for 32% of the time, Pallas kernels for 0%

commit v1 on v0

v1 whole, which is shorter than its diff:
```python
import functools
import math

import jax
import jax.numpy as jnp
import ml_dtypes
import numpy as np
from jax import lax
from jax.experimental import pallas as pl
from jax.experimental.pallas import tpu as pltpu
from jax.sharding import PartitionSpec as P

pair_index = ((0, 3, 4), (3, 1, 5), (4, 5, 2))
vmem_bytes = 56 * 1024 * 1024
by_rows = (((1,), (1,)), ((), ()))


def params():
    return pltpu.CompilerParams(vmem_limit_bytes=vmem_bytes)


def cost(flops, moved):
    return pl.CostEstimate(flops=flops, bytes_accessed=moved, transcendentals=0)


def angles(rows, columns, length):
    products = np.outer(np.arange(rows), np.arange(columns)) % length
    return 2.0 * math.pi / length * products


def halves(table):
    wide = np.asarray(table, np.float32)
    high = wide.astype(ml_dtypes.bfloat16)
    low = (wide - high.astype(np.float32)).astype(ml_dtypes.bfloat16)
    return jnp.asarray(high), jnp.asarray(low)


def split_two(data):
    high = data.astype(jnp.bfloat16)
    return high, (data - high.astype(jnp.float32)).astype(jnp.bfloat16)


def split_three(data):
    high = data.astype(jnp.bfloat16)
    rest = data - high.astype(jnp.float32)
    middle = rest.astype(jnp.bfloat16)
    return high, middle, (rest - middle.astype(jnp.float32)).astype(jnp.bfloat16)


def dot_rows(left, right):
    return lax.dot_general(left, right, by_rows, preferred_element_type=jnp.float32)


def dot_rows_split(table_high, table_low, data):
    high, low = split_two(data)
    return (
        dot_rows(table_high, high) + dot_rows(table_high, low) + dot_rows(table_low, high)
    )


def flat_fft(values, times):
    length = len(values)
    if length == 1:
        return values
    even = flat_fft(values[0::2], times)
    odd = flat_fft(values[1::2], times)
    lower, upper = [], []
    for k in range(length // 2):
        turned = times(odd[k], k, length)
        lower.append(jax.tree.map(lambda a, b: a + b, even[k], turned))
        upper.append(jax.tree.map(lambda a, b: a - b, even[k], turned))
    return lower + upper


def times_pair(value, k, length):
    real, imag = value
    if k == 0:
        return value
    if 4 * k == length:
        return (imag, -real)
    cos_k = math.cos(2.0 * math.pi * k / length)
    sin_k = math.sin(2.0 * math.pi * k / length)
    return (real * cos_k + imag * sin_k, imag * cos_k - real * sin_k)


def pack_kernel(devices, per_owner, with_slots, count, owner_col, owner_row, slot_row, tiles, out):
    listed = owner_row.shape[1]
    live_count = count[0]
    owners = owner_row[...]
    sender = lax.broadcasted_iota(jnp.int32, (listed, listed), 0)
    reader = lax.broadcasted_iota(jnp.int32, (listed, listed), 1)
    earlier = (owner_col[...] == owners) & (sender < reader) & (sender < live_count)
    rank = jnp.sum(jnp.where(earlier, 1.0, 0.0), axis=0, keepdims=True).astype(jnp.int32)
    live = lax.broadcasted_iota(jnp.int32, (1, listed), 1) < live_count
    target = jnp.where(live, owners * per_owner + rank, -1)
    places = lax.broadcasted_iota(jnp.int32, (devices * per_owner, listed), 0)
    chosen = jnp.where(places == target, 1.0, 0.0).astype(jnp.bfloat16)
    for comp in range(tiles.shape[1]):
        parts = [part for r in range(2) for part in split_three(tiles[r, comp])]
        got = jnp.dot(
            chosen, jnp.concatenate(parts, axis=1), preferred_element_type=jnp.float32
        )
        for r in range(2):
            one = got[:, 384 * r : 384 * r + 384]
            whole = (one[:, :128] + one[:, 128:256]) + one[:, 256:]
            out[comp, :, r * per_owner : (r + 1) * per_owner, :] = whole.reshape(
                devices, per_owner, 128
            )
    if with_slots:
        named = slot_row[...] + 1
        owner_at = lax.broadcasted_iota(jnp.int32, (devices, listed), 0)
        mine = (owner_at == owners) & live
        rank_at = lax.broadcasted_iota(jnp.int32, (128, listed), 0)
        ranked = jnp.where(rank_at == rank, 1.0, 0.0).astype(jnp.bfloat16)
        coarse = jnp.where(mine, (named >> 5).astype(jnp.float32), 0.0).astype(jnp.bfloat16)
        fine = jnp.where(mine, (named & 31).astype(jnp.float32), 0.0).astype(jnp.bfloat16)
        slots = 32.0 * dot_rows(coarse, ranked) + dot_rows(fine, ranked) - 1.0
        out[0, :, 2 * per_owner : 2 * per_owner + 8, :] = jnp.broadcast_to(
            slots[:, None, :], (devices, 8, 128)
        )


def pack(tiles, owner_col, owner_row, slot_row, count, devices, per_owner, with_slots):
    comps, listed = tiles.shape[1], tiles.shape[2]
    rows = 2 * per_owner + (8 if with_slots else 0)
    return pl.pallas_call(
        functools.partial(pack_kernel, devices, per_owner, with_slots),
        out_shape=jax.ShapeDtypeStruct((comps, devices, rows, 128), jnp.float32),
        in_specs=[pl.BlockSpec(memory_space=pltpu.SMEM)]
        + [pl.BlockSpec(memory_space=pltpu.VMEM)] * 4,
        out_specs=pl.BlockSpec(memory_space=pltpu.VMEM),
        compiler_params=params(),
        cost_estimate=cost(
            comps * devices * per_owner * listed * 768 * 2, comps * devices * rows * 1024
        ),
    )(count, owner_col, owner_row, slot_row, tiles)


def slab_kernel(
    x_local, blocks, per_owner, slots, data, table_high, table_low, twist, out, slab, turned
):
    devices = data.shape[0]
    entries = devices * per_owner
    wide = 2 * x_local
    slot = slots[...]
    shift = blocks.bit_length() - 1
    landing = jnp.where(slot >= 0, (slot & (blocks - 1)) * x_local + (slot >> shift), -1)
    parts = []
    for r in range(2):
        arrived = data[:, r * per_owner : (r + 1) * per_owner, :].reshape(entries, 128)
        parts.extend(split_two(arrived))
    parts = jnp.concatenate(parts, axis=1)
    for start in range(0, blocks * x_local, 256):
        place = start + lax.broadcasted_iota(jnp.int32, (256, entries), 0)
        chosen = jnp.where(place == landing, 1.0, 0.0).astype(jnp.bfloat16)
        got = jnp.dot(chosen, parts, preferred_element_type=jnp.float32)
        for r in range(2):
            slab[r, start : start + 256, :] = (
                got[:, 256 * r : 256 * r + 128] + got[:, 256 * r + 128 : 256 * r + 256]
            )

    @pl.loop(0, x_local // 8)
    def _(step):
        at = pl.multiple_of(step * 8, 8)
        values = [
            tuple(slab[r, pl.ds(t * x_local + at, 8), :] for r in range(2))
            for t in range(blocks)
        ]
        waves = flat_fft(values, times_pair)
        for k in range(blocks):
            real, imag = waves[k]
            cos_k, sin_k = twist[0, k : k + 1, :], twist[1, k : k + 1, :]
            new_real = real * cos_k + imag * sin_k
            new_imag = imag * cos_k - real * sin_k
            first = pl.ds(k * wide + at, 8)
            second = pl.ds(k * wide + x_local + at, 8)
            turned[first, :128] = new_real
            turned[first, 128:] = new_imag
            turned[second, :128] = new_imag
            turned[second, 128:] = -new_real

    for k in range(blocks):
        moved = dot_rows_split(
            table_high[...], table_low[...], turned[k * wide : (k + 1) * wide, :]
        )
        out[pl.ds(k, 128, stride=blocks), :] = moved


def slab_waves(slots, data, x_local, blocks, per_owner):
    y_cells = blocks * 128
    fine = angles(128, 128, 128)
    table = np.concatenate([np.cos(fine), np.sin(fine)], axis=1)
    twist_angle = angles(blocks, 128, y_cells)
    twist = np.stack([np.cos(twist_angle), np.sin(twist_angle)]).astype(np.float32)
    entries = data.shape[0] * per_owner
    return pl.pallas_call(
        functools.partial(slab_kernel, x_local, blocks, per_owner),
        out_shape=jax.ShapeDtypeStruct((y_cells, 2 * x_local), jnp.float32),
        in_specs=[pl.BlockSpec(memory_space=pltpu.VMEM)] * 5,
        out_specs=pl.BlockSpec(memory_space=pltpu.VMEM),
        scratch_shapes=[
            pltpu.VMEM((2, blocks * x_local, 128), jnp.float32),
            pltpu.VMEM((blocks * 2 * x_local, 256), jnp.float32),
        ],
        compiler_params=params(),
        cost_estimate=cost(
            blocks * x_local * entries * 512 * 2 + y_cells * x_local * 256 * 12,
            data.size * 4 + y_cells * x_local * 8,
        ),
    )(slots, data, *halves(table), jnp.asarray(twist))


def swap_parts(value, x_local):
    if 2 * x_local == 128:
        return pltpu.roll(value, x_local, 1)
    return jnp.concatenate([value[:, x_local:], value[:, :x_local]], axis=1)


def x_kernel(
    devices, x_local, y_local, data, twist, table_high, table_low, out, turned, columns
):
    wide = 2 * x_local
    lane = lax.broadcasted_iota(jnp.int32, (1, wide), 1)
    sign = jnp.where(lane < x_local, 1.0, -1.0)

    def times(value, k, length):
        if k == 0:
            return value
        swapped = swap_parts(value, x_local) * sign
        if 4 * k == length:
            return swapped
        cos_k = math.cos(2.0 * math.pi * k / length)
        sin_k = math.sin(2.0 * math.pi * k / length)
        return value * cos_k + swapped * sin_k

    @pl.loop(0, y_local // 8)
    def _(step):
        at = pl.multiple_of(step * 8, 8)
        values = [data[pl.ds(o * y_local + at, 8), :] for o in range(devices)]
        waves = flat_fft(values, times)
        for k in range(devices):
            swapped = swap_parts(waves[k], x_local)
            new = waves[k] * twist[0, k : k + 1, :] + swapped * twist[1, k : k + 1, :]
            turned[k, pl.ds(at, 8), :] = new
            turned[k, pl.ds(y_local + at, 8), :] = swap_parts(new, x_local) * sign

    for k in range(devices):
        columns[pl.ds(k, x_local, stride=devices), :] = dot_rows_split(
            table_high[...], table_low[...], turned[k]
        )
    for start in range(0, devices * x_local, 128):
        block = columns[start : start + 128, :].T
        out[0, :, start : start + 128] = block[:y_local]
        out[1, :, start : start + 128] = block[y_local:]


def x_waves(data, devices, x_local, y_local, y_cells):
    x_cells = devices * x_local
    fine = angles(x_local, x_local, x_local)
    scale = 1.0 / math.sqrt(x_cells * y_cells)
    table = np.concatenate([np.cos(fine), np.sin(fine)], axis=1) * scale
    angle = angles(devices, x_local, x_cells)
    cos_a, sin_a = np.cos(angle), np.sin(angle)
    twist = np.stack(
        [np.concatenate([cos_a, cos_a], axis=1), np.concatenate([sin_a, -sin_a], axis=1)]
    ).astype(np.float32)
    return pl.pallas_call(
        functools.partial(x_kernel, devices, x_local, y_local),
        out_shape=jax.ShapeDtypeStruct((2, y_local, x_cells), jnp.float32),
        in_specs=[pl.BlockSpec(memory_space=pltpu.VMEM)] * 4,
        out_specs=pl.BlockSpec(memory_space=pltpu.VMEM),
        scratch_shapes=[
            pltpu.VMEM((devices, 2 * y_local, 2 * x_local), jnp.float32),
            pltpu.VMEM((x_cells, 2 * y_local), jnp.float32),
        ],
        compiler_params=params(),
        cost_estimate=cost(x_cells * y_local * x_local * 24, x_cells * y_local * 16),
    )(data, jnp.asarray(twist), *halves(table))


def mix_kernel(green, first, second, third, out):
    waves = [(one[0], one[1]) for one in (first, second, third)]
    for row in range(3):
        real_sum = imag_sum = None
        for col in range(3):
            entry = pair_index[row][col]
            green_real, green_imag = green[0, entry], green[1, entry]
            real, imag = waves[col]
            real_term = green_real * real - green_imag * imag
            imag_term = green_real * imag + green_imag * real
            real_sum = real_term if real_sum is None else real_sum + real_term
            imag_sum = imag_term if imag_sum is None else imag_sum + imag_term
        out[0, row] = real_sum
        out[1, row] = imag_sum


def mix(green, waves):
    y_local, x_cells = green.shape[2], green.shape[3]
    step = 256
    wave_spec = pl.BlockSpec((2, y_local, step), lambda i: (0, 0, i))
    return pl.pallas_call(
        mix_kernel,
        grid=(x_cells // step,),
        out_shape=jax.ShapeDtypeStruct((2, 3, y_local, x_cells), jnp.float32),
        in_specs=[pl.BlockSpec((2, 6, y_local, step), lambda i: (0, 0, 0, i))] + [wave_spec] * 3,
        out_specs=pl.BlockSpec((2, 3, y_local, step), lambda i: (0, 0, 0, i)),
        compiler_params=params(),
        cost_estimate=cost(72 * y_local * x_cells, 96 * y_local * x_cells),
    )(green, *waves)


def exchange(data):
    return lax.all_to_all(data, ("gx", "gy"), split_axis=0, concat_axis=0, tiled=True)


def per_device(tiles, tile_owner, tile_slot, tile_count, green):
    devices = lax.axis_size("gx") * lax.axis_size("gy")
    tile_total, tile_len = tiles.shape[2], tiles.shape[3]
    planes, y_local, x_cells = green.shape[2:]
    y_cells = y_local * devices
    x_local = x_cells // devices
    blocks = y_cells // tile_len
    per_owner = max(2, 2 * tile_total // devices)
    assert planes == 1 and tile_len == 128
    lists = (tile_owner, tile_owner.reshape(1, tile_total), tile_slot.reshape(1, tile_total))
    lists = lists + (tile_count,)
    head = pack(tiles[:, :1], *lists, devices, per_owner, True)
    tail = pack(tiles[:, 1:], *lists, devices, per_owner, False)
    arrived = [exchange(head[0]), exchange(tail[0]), exchange(tail[1])]
    slots = arrived[0][:, 2 * per_owner, :per_owner].reshape(1, devices * per_owner)
    slots = slots.astype(jnp.int32)
    waves = []
    for comp in range(3):
        ready = slab_waves(slots, arrived[comp], x_local, blocks, per_owner)
        moved = exchange(ready.reshape(devices, y_local, 2 * x_local))
        moved = moved.reshape(devices * y_local, 2 * x_local)
        waves.append(x_waves(moved, devices, x_local, y_local, y_cells))
    mixed = mix(green.reshape(2, 6, y_local, x_cells), waves)
    return mixed.reshape(2, 3, planes, y_local, x_cells)


def solution(mesh):
    in_specs = (
        P(None, None, ("gx", "gy"), None),
        P(("gx", "gy"), None),
        P(("gx", "gy")),
        P(("gx", "gy")),
        P(None, None, None, ("gx", "gy"), None),
    )
    out_specs = P(None, None, None, ("gx", "gy"), None)
    return jax.shard_map(
        per_device, mesh=mesh, in_specs=in_specs, out_specs=out_specs, check_vma=False
    )
```

time: 958 us -> 221 us (0.23)
  matrix products: 376 us -> 0 us
  other arithmetic: 342 us -> 0.05 us
  local copies, waits for them, and re-layouts: 105 us -> 10.4 us
  Pallas kernels: 0 us -> 57.4 us
  blocking collectives: 0 us -> 33 us
    dot_general x8 -> x0, matrix products: 376 us -> none  [the longest x4 298 us: across_sources(): lax.dot_general(data, table, (((0, 4), (0, 1)), ((), ())), precision=lax....]
    dot_general x4 -> x0, other arithmetic: 248 us -> none  [table_first(): lax.dot_general(table, data, (((1,), (1,)), ((), ())), precision=lax.Prec...]
    scatter-add x1 -> x0, other arithmetic: 85.2 us -> none  [per_device(): slab_field = slab_field.at[:, :, landing, :].add(arriving, mode='drop')]
    pallas_call x0 -> x9, Pallas kernels: none -> 57.4 us  [the longest x3 26.4 us: x_waves(): pl.pallas_call(functools.partial(x_kernel, devices, x_local, y_local), ou...]
    scatter x2 -> x0, local copies, waits for them, and re-layouts: 49.7 us -> none  [the longest x1 47.1 us: per_device(): outgoing = outgoing.at[:, :, target, :].set(tiles, mode='drop')]
    all_to_all x0 -> x1, blocking collectives: none -> 33 us  [exchange(): lax.all_to_all(data, ('gx', 'gy'), split_axis=0, concat_axis=0, tiled=True)]
    slice x4 -> x2, local copies, waits for them, and re-layouts: 27.3 us -> 4.14 us  [the longest x1 2.26 us: per_device(): tail = pack(tiles[:, 1:], *lists, devices, per_owner, False)]
    another operation x7 -> x0, local copies, waits for them, and re-layouts: 16.5 us -> none
  transfers between devices with their start and end apart: 3 -> 5, of which waited for: 1 -> 5; matrix products, arithmetic and copies ran while one was open for 32% -> 1% of each run, Pallas kernels for 0% -> 16%
where the time goes in v1:
time: 221 us; the launch traced here: 220 us
  waiting for transfers between devices  99.1 us (45%)
  Pallas kernels  57.4 us (26%)
  blocking collectives  33 us (15%)
  starting transfers between devices  18.8 us (9%)
  local copies, waits for them, and re-layouts  10.4 us (5%)
    all_to_all x5, waiting for transfers between devices, exchange(): lax.all_to_all(data, ('gx', 'gy'), split_axis=0, concat_axis=0, tiled=True)  99.1 us
    all_to_all x1, blocking collectives, exchange(): lax.all_to_all(data, ('gx', 'gy'), split_axis=0, concat_axis=0, tiled=True)  33 us
    pallas_call x3, Pallas kernels, x_waves(): pl.pallas_call(functools.partial(x_kernel, devices, x_local, y_local), ou...  26.4 us
    all_to_all x5, starting transfers between devices, exchange(): lax.all_to_all(data, ('gx', 'gy'), split_axis=0, concat_axis=0, tiled=True)  18.8 us
    pallas_call x3, Pallas kernels, slab_waves(): pl.pallas_call(functools.partial(slab_kernel, x_local, blocks, per_owner)...  14.9 us
    pallas_call x2, Pallas kernels, pack(): pl.pallas_call(functools.partial(pack_kernel, devices, per_owner, with_sl...  8.09 us
    pallas_call x1, Pallas kernels, mix(): pl.pallas_call(mix_kernel, grid=(x_cells // step,), out_shape=jax.ShapeDt...  7.96 us
  transfers between devices with their start and end apart: 5, of which 5 were waited for; matrix products, arithmetic and copies ran while one was open for 1% of the time, Pallas kernels for 16%

profile of v1, /device:TPU:0, one launch (start us, length us, event | category | flops | bytes accessed | tf_op | source)
XLA Modules:
  0.0 219.6 jit_solution(9315898607982600347)
XLA Ops:
  0.7 1.5 copy.24.owner_col
  2.2 2.3 %slice.17.tiles = f32[2,2,512,128]{3,2,1,0:T(8,128)} slice(f32[2,3,512,128]{3,2,1,0:T(8,128)} %param.23), slice={[0:2], [1:3], [0:512], [0:128]} | slice | bytes 2097152 | tf_op jit(solution)/shard_map/slice | solution.py:328
  4.5 4.6 %shard_map.220 = f32[2,32,64,128]{3,2,1,0:T(8,128)} custom-call(s32[1]{0:T(128)S(6)} %copy.27.count, s32[512,1]{1,0:T(8,128)} %copy.24.owner_col, s32[1,512]{1,0:T(1,128)} %bitcast.25, s32[1,512]{1,0:T(1,128)} %bitcast.27, f32[2,2,512,128]{3,2,1,0:T(8,128)} %slice.17.tiles), custom_call_target="tpu_custom_call" | custom-call | flops 1610612736 | bytes 4194304 | tf_op jit(solution)/shard_map/pallas_call | solution.py:126
  9.1 3.1 %slice_bitcast_fusion = (f32[32,64,128]{2,1,0:T(8,128)}, f32[32,64,128]{2,1,0:T(8,128)}) fusion(f32[2,32,64,128]{3,2,1,0:T(8,128)} %shard_map.220), kind=kLoop, calls=%fused_computation | loop fusion | bytes 4194304 | tf_op jit(solution)/shard_map/squeeze | solution.py:329
  12.2 7.3 %all-to-all-start.4 = ((f32[32,64,128]{2,1,0:T(8,128)}), f32[32,64,128]{2,1,0:T(8,128)S(1)}, u32[]{:S(2)}, u32[]{:S(2)}) async-start(f32[32,64,128]{2,1,0:T(8,128)} %get-tuple-element.5), calls=%async_computation.4 | async-start | bytes 2097152 | tf_op jit(solution)/shard_map/all_to_all | solution.py:313
  19.5 1.9 slice.15.tiles
  21.4 3.4 %shard_map.217 = f32[1,32,72,128]{3,2,1,0:T(8,128)} custom-call(s32[1]{0:T(128)S(6)} %copy.27.count, s32[512,1]{1,0:T(8,128)} %copy.24.owner_col, s32[1,512]{1,0:T(1,128)} %bitcast.26, s32[1,512]{1,0:T(1,128)} %bitcast.28, f32[2,1,512,128]{3,2,1,0:T(8,128)} %slice.15.tiles), custom_call_target="tpu_custom_call" | custom-call | flops 805306368 | bytes 2359296 | tf_op jit(solution)/shard_map/pallas_call | solution.py:126
  24.8 22.3 %all-to-all-done.4.data = f32[32,64,128]{2,1,0:T(8,128)S(1)} async-done(((f32[32,64,128]{2,1,0:T(8,128)}), f32[32,64,128]{2,1,0:T(8,128)S(1)}, u32[]{:S(2)}, u32[]{:S(2)}) %all-to-all-start.4) | async-done | bytes 1048608 | tf_op jit(solution)/shard_map/all_to_all | solution.py:313
  47.1 0.0 copy-start.4
  47.1 33.0 %all_to_all.30.data = f32[32,72,128]{2,1,0:T(8,128)S(1)} all-to-all(f32[32,72,128]{2,1,0:T(8,128)} %bitcast.21), channel_id=1, replica_groups=mesh['gx'=4,'gy'=8] {'gx','gy'}, dimensions={0} | all-to-all | bytes 2359296 | tf_op jit(solution)/shard_map/all_to_all | solution.py:313
  80.1 0.0 copy-start.3
  80.1 0.0 copy-done.4
  80.2 3.4 %all-to-all-start.2 = ((f32[32,64,128]{2,1,0:T(8,128)}), f32[32,64,128]{2,1,0:T(8,128)}, u32[]{:S(2)}, u32[]{:S(2)}) async-start(f32[32,64,128]{2,1,0:T(8,128)} %get-tuple-element.6), calls=%async_computation.2 | async-start | bytes 2097152 | tf_op jit(solution)/shard_map/all_to_all | solution.py:313
  83.5 0.1 fusion
  83.6 0.7 convert_element_type.6.slots
  84.3 0.0 copy-done.3
  84.3 5.0 %shard_map.218 = f32[2048,128]{1,0:T(8,128)} custom-call(s32[1,1024]{1,0:T(1,128)} %convert_element_type.6.slots, f32[32,72,128]{2,1,0:T(8,128)} %copy-done.3, bf16[128,256]{1,0:T(8,128)(2,1)} %constant.12.clone.table_high, bf16[128,256]{1,0:T(8,128)(2,1)} %constant.13.clone.table_low, f32[2,16,128]{2,1,0:T(8,128)} %constant.14.clone.twist), custom_call_target="tpu_custom_call" | custom-call | flops 1476395008 | bytes 2228224 | tf_op jit(solution)/shard_map/pallas_call | solution.py:196
  89.3 21.8 %all-to-all-done.2.data = f32[32,64,128]{2,1,0:T(8,128)} async-done(((f32[32,64,128]{2,1,0:T(8,128)}), f32[32,64,128]{2,1,0:T(8,128)}, u32[]{:S(2)}, u32[]{:S(2)}) %all-to-all-start.2) | async-done | bytes 1048608 | tf_op jit(solution)/shard_map/all_to_all | solution.py:313
  111.1 2.6 %all-to-all-start.1 = ((f32[32,64,128]{2,1,0:T(8,128)}), f32[32,64,128]{2,1,0:T(8,128)S(1)}, u32[]{:S(2)}, u32[]{:S(2)}) async-start(f32[32,64,128]{2,1,0:T(8,128)} %bitcast.24), calls=%async_computation.1 | async-start | bytes 2097152 | tf_op jit(solution)/shard_map/all_to_all | solution.py:313
  113.8 5.0 %shard_map.223 = f32[2048,128]{1,0:T(8,128)} custom-call(s32[1,1024]{1,0:T(1,128)} %convert_element_type.6.slots, f32[32,64,128]{2,1,0:T(8,128)} %copy-done.4, bf16[128,256]{1,0:T(8,128)(2,1)} %constant.12.clone.table_high, bf16[128,256]{1,0:T(8,128)(2,1)} %constant.13.clone.table_low, f32[2,16,128]{2,1,0:T(8,128)} %constant.14.clone.twist), custom_call_target="tpu_custom_call" | custom-call | flops 1476395008 | bytes 2097152 | tf_op jit(solution)/shard_map/pallas_call | solution.py:196
  118.7 22.6 %all-to-all-done.1 = f32[32,64,128]{2,1,0:T(8,128)S(1)} async-done(((f32[32,64,128]{2,1,0:T(8,128)}), f32[32,64,128]{2,1,0:T(8,128)S(1)}, u32[]{:S(2)}, u32[]{:S(2)}) %all-to-all-start.1) | async-done | bytes 1048608 | tf_op jit(solution)/shard_map/all_to_all | solution.py:313
  141.3 0.0 copy-start
  141.3 2.6 %all-to-all-start.5 = ((f32[32,64,128]{2,1,0:T(8,128)}), f32[32,64,128]{2,1,0:T(8,128)S(1)}, u32[]{:S(2)}, u32[]{:S(2)}) async-start(f32[32,64,128]{2,1,0:T(8,128)} %bitcast.23), calls=%async_computation.5 | async-start | bytes 2097152 | tf_op jit(solution)/shard_map/all_to_all | solution.py:313
  144.0 5.0 %shard_map.221 = f32[2048,128]{1,0:T(8,128)} custom-call(s32[1,1024]{1,0:T(1,128)} %convert_element_type.6.slots, f32[32,64,128]{2,1,0:T(8,128)} %all-to-all-done.2.data, bf16[128,256]{1,0:T(8,128)(2,1)} %constant.12.clone.table_high, bf16[128,256]{1,0:T(8,128)(2,1)} %constant.13.clone.table_low, f32[2,16,128]{2,1,0:T(8,128)} %constant.14.clone.twist), custom_call_target="tpu_custom_call" | custom-call | flops 1476395008 | bytes 2097152 | tf_op jit(solution)/shard_map/pallas_call | solution.py:196
  149.0 0.0 copy-done
  149.0 22.6 %all-to-all-done.5 = f32[32,64,128]{2,1,0:T(8,128)S(1)} async-done(((f32[32,64,128]{2,1,0:T(8,128)}), f32[32,64,128]{2,1,0:T(8,128)S(1)}, u32[]{:S(2)}, u32[]{:S(2)}) %all-to-all-start.5) | async-done | bytes 1048608 | tf_op jit(solution)/shard_map/all_to_all | solution.py:313
  171.6 0.0 copy-start.1
  171.6 2.8 %all-to-all-start.3 = ((f32[32,64,128]{2,1,0:T(8,128)}), f32[32,64,128]{2,1,0:T(8,128)S(1)}, u32[]{:S(2)}, u32[]{:S(2)}) async-start(f32[32,64,128]{2,1,0:T(8,128)} %bitcast.22), calls=%async_computation.3 | async-start | bytes 2097152 | tf_op jit(solution)/shard_map/all_to_all | solution.py:313
  174.4 8.8 %shard_map.219.first = f32[2,64,2048]{2,1,0:T(8,128)} custom-call(f32[2048,128]{1,0:T(8,128)} %bitcast.18, f32[2,32,128]{2,1,0:T(8,128)} %constant.15.clone.twist, bf16[64,128]{1,0:T(8,128)(2,1)} %constant.16.clone.table_high, bf16[64,128]{1,0:T(8,128)(2,1)} %constant.17.clone.table_low), custom_call_target="tpu_custom_call" | custom-call | flops 201326592 | bytes 2097152 | tf_op jit(solution)/shard_map/pallas_call | solution.py:267
  183.3 0.0 copy-done.1
  183.3 8.8 %shard_map.224.third = f32[2,64,2048]{2,1,0:T(8,128)} custom-call(f32[2048,128]{1,0:T(8,128)} %bitcast.19, f32[2,32,128]{2,1,0:T(8,128)} %constant.15.clone.twist, bf16[64,128]{1,0:T(8,128)(2,1)} %constant.16.clone.table_high, bf16[64,128]{1,0:T(8,128)(2,1)} %constant.17.clone.table_low), custom_call_target="tpu_custom_call" | custom-call | flops 201326592 | bytes 2097152 | tf_op jit(solution)/shard_map/pallas_call | solution.py:267
  192.0 9.8 %all-to-all-done.3 = f32[32,64,128]{2,1,0:T(8,128)S(1)} async-done(((f32[32,64,128]{2,1,0:T(8,128)}), f32[32,64,128]{2,1,0:T(8,128)S(1)}, u32[]{:S(2)}, u32[]{:S(2)}) %all-to-all-start.3) | async-done | bytes 1048608 | tf_op jit(solution)/shard_map/all_to_all | solution.py:313
  201.8 0.0 copy-start.2
  201.8 1.0 copy-done.2
  202.8 8.8 %shard_map.222.second = f32[2,64,2048]{2,1,0:T(8,128)} custom-call(f32[2048,128]{1,0:T(8,128)} %bitcast.20, f32[2,32,128]{2,1,0:T(8,128)} %constant.15.clone.twist, bf16[64,128]{1,0:T(8,128)(2,1)} %constant.16.clone.table_high, bf16[64,128]{1,0:T(8,128)(2,1)} %constant.17.clone.table_low), custom_call_target="tpu_custom_call" | custom-call | flops 201326592 | bytes 2097152 | tf_op jit(solution)/shard_map/pallas_call | solution.py:267
  211.6 8.0 %shard_map.225 = f32[2,3,64,2048]{3,2,1,0:T(8,128)} custom-call(f32[2,6,64,2048]{3,2,1,0:T(8,128)} %bitcast.17, f32[2,64,2048]{2,1,0:T(8,128)} %shard_map.219.first, f32[2,64,2048]{2,1,0:T(8,128)} %shard_map.222.second, f32[2,64,2048]{2,1,0:T(8,128)} %shard_map.224.third), custom_call_target="tpu_custom_call" | custom-call | flops 9437184 | bytes 12582912 | tf_op jit(solution)/shard_map/pallas_call | solution.py:301
Async XLA Ops:
  12.2 34.9 %all-to-all-start.4 = ((f32[32,64,128]{2,1,0:T(8,128)}), f32[32,64,128]{2,1,0:T(8,128)S(1)}, u32[]{:S(2)}, u32[]{:S(2)}) async-start(f32[32,64,128]{2,1,0:T(8,128)} %get-tuple-element.5), calls=%async_computation.4 | async-start | bytes 2097152 | tf_op jit(solution)/shard_map/all_to_all | solution.py:313
  47.1 33.1 %copy-start.4 = (f32[32,64,128]{2,1,0:T(8,128)}, f32[32,64,128]{2,1,0:T(8,128)S(1)}, u32[]{:S(2)}) copy-start(f32[32,64,128]{2,1,0:T(8,128)S(1)} %all-to-all-done.4.data) | copy-start | bytes 3145732
  80.1 4.1 %copy-start.3 = (f32[32,72,128]{2,1,0:T(8,128)}, f32[32,72,128]{2,1,0:T(8,128)S(1)}, u32[]{:S(2)}) copy-start(f32[32,72,128]{2,1,0:T(8,128)S(1)} %all_to_all.30.data) | copy-start | bytes 3538948
  80.2 31.0 %all-to-all-start.2 = ((f32[32,64,128]{2,1,0:T(8,128)}), f32[32,64,128]{2,1,0:T(8,128)}, u32[]{:S(2)}, u32[]{:S(2)}) async-start(f32[32,64,128]{2,1,0:T(8,128)} %get-tuple-element.6), calls=%async_computation.2 | async-start | bytes 2097152 | tf_op jit(solution)/shard_map/all_to_all | solution.py:313
  111.1 30.2 %all-to-all-start.1 = ((f32[32,64,128]{2,1,0:T(8,128)}), f32[32,64,128]{2,1,0:T(8,128)S(1)}, u32[]{:S(2)}, u32[]{:S(2)}) async-start(f32[32,64,128]{2,1,0:T(8,128)} %bitcast.24), calls=%async_computation.1 | async-start | bytes 2097152 | tf_op jit(solution)/shard_map/all_to_all | solution.py:313
  141.3 7.6 %copy-start = (f32[32,64,128]{2,1,0:T(8,128)}, f32[32,64,128]{2,1,0:T(8,128)S(1)}, u32[]{:S(2)}) copy-start(f32[32,64,128]{2,1,0:T(8,128)S(1)} %all-to-all-done.1) | copy-start | bytes 3145732
  141.3 30.2 %all-to-all-start.5 = ((f32[32,64,128]{2,1,0:T(8,128)}), f32[32,64,128]{2,1,0:T(8,128)S(1)}, u32[]{:S(2)}, u32[]{:S(2)}) async-start(f32[32,64,128]{2,1,0:T(8,128)} %bitcast.23), calls=%async_computation.5 | async-start | bytes 2097152 | tf_op jit(solution)/shard_map/all_to_all | solution.py:313
  171.6 11.7 %copy-start.1 = (f32[32,64,128]{2,1,0:T(8,128)}, f32[32,64,128]{2,1,0:T(8,128)S(1)}, u32[]{:S(2)}) copy-start(f32[32,64,128]{2,1,0:T(8,128)S(1)} %all-to-all-done.5) | copy-start | bytes 3145732
  171.6 30.2 %all-to-all-start.3 = ((f32[32,64,128]{2,1,0:T(8,128)}), f32[32,64,128]{2,1,0:T(8,128)S(1)}, u32[]{:S(2)}, u32[]{:S(2)}) async-start(f32[32,64,128]{2,1,0:T(8,128)} %bitcast.22), calls=%async_computation.3 | async-start | bytes 2097152 | tf_op jit(solution)/shard_map/all_to_all | solution.py:313
  201.8 1.0 copy-start.2
